TPU v7x, 128 devices: a whole 4x4x4 slice. The times are simulated.
128 devices in a mesh: ha: 16 (over x_hi, z, core), wa: 8 (over y, x_lo).
Axes of the slice: x: 4 (x_hi: 2, x_lo: 2; x = x_hi * 2 + x_lo), y: 4, z: 4, core: 2. Of those that a mesh axis runs over, the one named last changes fastest.
Arguments:
- queries: bfloat16 [4, 192, 64, 1536], P(None, 'ha', 'wa'), may hold values from -5 to 5
- key_heads: bfloat16 [4, 192, 64, 1536], P(None, 'ha', 'wa'), may hold values from -5 to 5
- value_heads: bfloat16 [4, 192, 64, 1536], P(None, 'ha', 'wa'), may hold values from -6 to 6
- out_grad: bfloat16 [4, 192, 64, 1536], P(None, 'ha', 'wa'), may hold values from -6 to 6
- reach_tiles: int32 [48, 16, 4], P('ha', 'wa'), may hold values from 0 to 1
Outputs:
- attended: bfloat16 [4, 192, 64, 1536], P(None, 'ha', 'wa')
- query_grad: bfloat16 [4, 192, 64, 1536], P(None, 'ha', 'wa')
- key_grad: bfloat16 [4, 192, 64, 1536], P(None, 'ha', 'wa')
- value_grad: bfloat16 [4, 192, 64, 1536], P(None, 'ha', 'wa')
All inputs are finite; a program needn't handle non-finite values.
Results may differ from a plain program's by a relative error of at most 0.03.
Values may be sent and summed in bfloat16 or wider, within the bound.
A program may use at most 192 MiB of HBM per device.

v0:
```python
import functools
import math

import jax
import jax.numpy as jnp
from jax import lax
from jax.experimental import pallas as pl
from jax.experimental.pallas import tpu as pltpu
from jax.sharding import PartitionSpec as P

HEADS = 12
TS = 4
D = 128
MESH = pl.DeviceIdType.MESH
AHEAD = 4
CORNERS_AHEAD = 2
NEGATIVE = -1e30
SCALE = 1.0 / math.sqrt(D)
LOG2E = 1.4426950408889634

F32 = jnp.float32
BF16 = jnp.bfloat16


def dot(a, b, ca, cb):
    return lax.dot_general(a, b, (((ca,), (cb,)), ((), ())), preferred_element_type=F32)


def kernel(
    size_a, size_w, reach, q_in, k_in, v_in, g_in, o_out, dq_out, dk_out, dv_out,
    kall, qg, pack, acc, own, g3s, g3r, g4s, g4r, ob, bias, perm, perm_t,
    in_sem, out_sem, ss1, rs1, ss2, rs2, ss3, rs3, ss4, rs4,
):
    half_a = size_a // 2
    ia = lax.axis_index("ha")
    iw = lax.axis_index("wa")
    has_u, has_d = ia > 0, ia < size_a - 1
    has_l, has_r = iw > 0, iw < size_w - 1
    up, down = (ia - 1, iw), (ia + 1, iw)
    left, right = (ia, iw - 1), (ia, iw + 1)
    sides = ((has_l, left), (has_r, right))
    ends = ((has_u, up), (has_d, down))
    crossed = (ia == half_a, ia == half_a - 1)

    def lanes(h):
        return pl.ds(pl.multiple_of(h * D, D), D)

    def load(h, n):
        src = (k_in, v_in, q_in, g_in)[n].at[:, :, :, lanes(h)]
        dst = kall.at[h, n, 2:6, 1:4] if n < 2 else qg.at[h, n - 2]
        return pltpu.make_async_copy(src, dst, in_sem.at[h, n])

    def store(h, n):
        dst = (o_out, dq_out, dk_out, dv_out)[n].at[:, :, :, lanes(h)]
        return pltpu.make_async_copy(ob.at[h, n], dst, out_sem.at[h, n])

    def remote(src, dst, ss, rs, dev):
        return pltpu.make_async_remote_copy(
            src_ref=src, dst_ref=dst, send_sem=ss, recv_sem=rs, device_id=dev, device_id_type=MESH
        )

    def col_copy(h, s, dev):
        lo = 6 - 6 * s
        return remote(
            pack.at[h, :, 2 * s : 2 * s + 2], kall.at[h, :, lo : lo + 2, 1:4], ss1.at[h, s], rs1.at[h, 1 - s], dev
        )

    def row_place(s, j):
        moved = crossed[s] & sides[j // 2][0]
        col = jnp.where(moved, iw + (2 * (j // 2) - 1), iw)
        return jnp.where(moved, (j + 2) % 4, j), (ia + (2 * s - 1), col)

    def row_there(s, j):
        return ends[s][0] if j in (1, 2) else ends[s][0] & sides[j // 2][0]

    def row_copy(h, s, j):
        slot, dev = row_place(s, j)
        src = pack.at[h, :, 2 * j - 2 : 2 * j, 2 * s] if j in (1, 2) else kall.at[h, :, 2 * j : 2 * j + 2, 1 + 2 * s]
        dst = kall.at[h, :, pl.ds(2 * slot, 2), 4 - 4 * s]
        return remote(src, dst, ss2.at[h, s, j], rs2.at[h, 1 - s, slot], dev)

    def send_rows(h, columns):
        for s in range(2):
            for j in columns:

                @pl.when(row_there(s, j))
                def _():
                    row_copy(h, s, j).start()

    def receive_row(h, s, j):
        @pl.when(row_there(s, j))
        def _():
            ref = kall.at[h, :, 2 * j : 2 * j + 2, 4 * s]
            remote(ref, ref, ss2.at[h, s, j], rs2.at[h, s, j], ends[s][1]).wait_recv()

    def grad_row_copy(h, s, half):
        moved = crossed[s] & sides[half][0]
        col = jnp.where(moved, iw + (2 * half - 1), iw)
        to = jnp.where(moved, 1 - half, half)
        return remote(
            g3s.at[h, s, half], g3r.at[h, 1 - s, to], ss3.at[h, s, half], rs3.at[h, 1 - s, to], (ia + (2 * s - 1), col)
        )

    def grad_col_copy(h, s, dev):
        return remote(g4s.at[h, s], g4r.at[h, 1 - s], ss4.at[h, s], rs4.at[h, 1 - s], dev)

    def send(copy, h, group):
        for s, (there, dev) in enumerate(group):

            @pl.when(there)
            def _():
                copy(h, s, dev).start()

    def receive(copy, h, group, s):
        there, dev = group[s]

        @pl.when(there)
        def _():
            copy(h, 1 - s, dev).wait_recv()

    def loop(body):
        lax.fori_loop(0, HEADS, lambda h, c: (body(h), c)[1], 0)

    def load_kv(h):
        load(h, 0).start()
        load(h, 1).start()

    def load_qg(h):
        load(h, 2).start()
        load(h, 3).start()

    loop(load_kv)
    loop(load_qg)

    barrier = pltpu.get_barrier_semaphore()
    greeted = sides + ends
    for s, row in ((0, ia - 1), (1, ia + 1)):
        greeted += ((crossed[s] & has_l, (row, iw - 1)), (crossed[s] & has_r, (row, iw + 1)))
    for there, dev in greeted:

        @pl.when(there)
        def _():
            pl.semaphore_signal(barrier, inc=1, device_id=dev, device_id_type=MESH)

    def packed_of(i):
        return ((i >> 2) & 1) * 64 + (i >> 5) * 16 + ((i >> 3) & 3) * 4 + (i & 3)

    first = lax.broadcasted_iota(jnp.int32, (128, 128), 0)
    second = lax.broadcasted_iota(jnp.int32, (128, 128), 1)
    perm[...] = jnp.where(packed_of(first) == second, 1.0, 0.0).astype(BF16)
    perm_t[...] = jnp.where(packed_of(second) == first, 1.0, 0.0).astype(BF16)

    for s, (there, _) in enumerate(sides):

        @pl.when(jnp.logical_not(there))
        def _():
            def fill(h):
                kall[h, :, 6 * s : 6 * s + 2] = jnp.zeros((2, 2, 5, 32, D), BF16)
                g4r[h, s] = jnp.zeros((2, 2, 3, 32, D), BF16)

            loop(fill)

    for s, (there, _) in enumerate(ends):

        @pl.when(jnp.logical_not(there))
        def _():
            def fill(h):
                kall[h, :, :, 4 * s] = jnp.zeros((2, 8, 32, D), BF16)

            loop(fill)

    count = sum(there.astype(jnp.int32) for there, _ in greeted)
    pl.semaphore_wait(barrier, count)

    def send_edges(h):
        load(h, 0).wait()
        load(h, 1).wait()
        for kv in range(2):
            for a in range(3):
                x = kall[h, kv, 2:6, a + 1].reshape(128, D)
                pack[h, kv, :, a] = dot(perm_t[...], x, 1, 0).astype(BF16).reshape(4, 32, D)
        send_rows(h, (1, 2))
        send(col_copy, h, sides)

    for h in range(AHEAD):
        send_edges(h)

    shape = (8, 3, 32, 128)
    unit = lax.broadcasted_iota(jnp.int32, shape, 0)
    drow = lax.broadcasted_iota(jnp.int32, shape, 1) - 1
    token = lax.broadcasted_iota(jnp.int32, shape, 2)
    query = lax.broadcasted_iota(jnp.int32, shape, 3)
    qcol = (query >> 2) & 1
    for a in range(3):
        own_col = (token >> 2) & 1
        if a != 1:
            own_col = jnp.where(drow == a - 1, (unit >> 1) - 1, own_col)
        kcol = jnp.where((unit >= 2) & (unit < 6), own_col, (unit >> 1) - 1)
        dcol = kcol - qcol
        acol = iw * 2 + kcol
        in_cols = (acol >= 0) & (acol < 2 * size_w)

        def of(n):
            return jnp.where(qcol == 0, reach[a, 0, n], reach[a, 1, n])

        arow = ia * 3 + a + drow
        ok = in_cols & (arow >= 0) & (arow < 3 * size_a)
        ok = ok & (drow >= -of(0)) & (drow <= of(1)) & (dcol >= -of(2)) & (dcol <= of(3))
        bias[a] = jnp.where(ok, 0.0, NEGATIVE).astype(F32).reshape(768, 128)

    def forward(h):
        receive(col_copy, h, sides, 0)
        receive(col_copy, h, sides, 1)
        send_rows(h, (0, 3))

    def attend(h, slot, a):
        kk = kall[h, 0, :, pl.ds(a, 3)].reshape(768, D)
        vv = kall[h, 1, :, pl.ds(a, 3)].reshape(768, D)
        q = qg[h, 0, :, a].reshape(128, D)
        g = qg[h, 1, :, a].reshape(128, D)
        s = dot(kk, q, 1, 1) * (SCALE * LOG2E) + bias[a]
        p = jnp.exp2(s - jnp.max(s, axis=0, keepdims=True))
        p = p * (1.0 / jnp.sum(p, axis=0, keepdims=True))
        low = p.astype(BF16)
        dp = dot(vv, g, 1, 1)
        delta = jnp.sum(p * dp, axis=0, keepdims=True)
        ds = (p * (dp - delta)).astype(BF16)
        ob[h, 0, :, a] = dot(low, vv, 0, 0).astype(BF16).reshape(4, 32, D)
        ob[h, 1, :, a] = (dot(ds, kk, 0, 0) * SCALE).astype(BF16).reshape(4, 32, D)
        acc[slot, 0, :, pl.ds(a, 3)] += dot(ds, q, 1, 0).reshape(8, 3, 32, D)
        acc[slot, 1, :, pl.ds(a, 3)] += dot(low, g, 1, 0).reshape(8, 3, 32, D)

    def reduce_rows(h, slot):
        for s, row in ((0, 1), (1, 3)):
            @pl.when(ends[s][0])
            def _():
                for half in range(2):
                    ref = g3r.at[h, s, half]
                    remote(ref, ref, ss3.at[h, s, half], rs3.at[h, s, half], ends[s][1]).wait_recv()
                acc[slot, :, 0:2, row] += g3r[h, s, 0, :, 0:2].astype(F32)
                acc[slot, :, 6:8, row] += g3r[h, s, 1, :, 2:4].astype(F32)
                for kv in range(2):
                    x = jnp.concatenate([g3r[h, s, 0, kv, 2:4], g3r[h, s, 1, kv, 0:2]]).reshape(128, D)
                    acc[slot, kv, 2:6, row] += dot(perm[...], x, 1, 0).reshape(4, 32, D)

        for s in range(2):
            g4s[h, s] = acc[slot, :, 6 * s : 6 * s + 2, 1:4].astype(BF16)
        send(grad_col_copy, h, sides)
        own[h] = acc[slot, :, 2:6, 1:4]

    for h in range(CORNERS_AHEAD):
        forward(h)

    def step(h):
        slot = h % 2

        @pl.when(h + CORNERS_AHEAD < HEADS)
        def _():
            forward(h + CORNERS_AHEAD)

        @pl.when(h + AHEAD < HEADS)
        def _():
            send_edges(h + AHEAD)

        load(h, 2).wait()
        load(h, 3).wait()
        for s in range(2):
            for j in range(4):
                receive_row(h, s, j)
        acc[slot] = jnp.zeros((2, 8, 5, 32, D), F32)
        lax.fori_loop(0, 3, lambda a, c: (attend(h, slot, a), c)[1], 0)
        store(h, 0).start()
        store(h, 1).start()
        for s in range(2):
            for half in range(2):
                g3s[h, s, half] = acc[slot, :, 4 * half : 4 * half + 4, 4 * s].astype(BF16)

            @pl.when(ends[s][0])
            def _():
                for half in range(2):
                    grad_row_copy(h, s, half).start()


        @pl.when(h >= 1)
        def _():
            reduce_rows(h - 1, 1 - slot)

    loop(step)
    reduce_rows(HEADS - 1, (HEADS - 1) % 2)

    def finish(h):
        for s in range(2):
            receive(grad_col_copy, h, sides, s)
        for kv in range(2):
            for a in range(3):
                x = g4r[h, :, kv, :, a].reshape(128, D)
                y = dot(perm[...], x, 1, 0) + own[h, kv, :, a].reshape(128, D)
                if kv == 0:
                    y = y * SCALE
                ob[h, 2 + kv, :, a] = y.astype(BF16).reshape(4, 32, D)
        store(h, 2).start()
        store(h, 3).start()

    loop(finish)

    def drain(h):
        for n in range(4):
            store(h, n).wait()
        for copy in (col_copy, grad_col_copy):
            for s, (there, dev) in enumerate(sides):

                @pl.when(there)
                def _():
                    copy(h, s, dev).wait_send()

        for s in range(2):
            for j in range(4):

                @pl.when(row_there(s, j))
                def _():
                    row_copy(h, s, j).wait_send()

            @pl.when(ends[s][0])
            def _():
                for half in range(2):
                    grad_row_copy(h, s, half).wait_send()

    loop(drain)


def per_device(size_a, size_w, queries, key_heads, value_heads, out_grad, reach_tiles):
    shape = queries.shape
    ins = [x.reshape(4, 3, 32, HEADS * D) for x in (queries, key_heads, value_heads, out_grad)]
    any_spec = pl.BlockSpec(memory_space=pl.ANY)
    pair = pltpu.SemaphoreType.DMA((HEADS, 2))
    outs = pl.pallas_call(
        functools.partial(kernel, size_a, size_w),
        out_shape=[jax.ShapeDtypeStruct((4, 3, 32, HEADS * D), BF16)] * 4,
        in_specs=[pl.BlockSpec(memory_space=pltpu.SMEM)] + [any_spec] * 4,
        out_specs=[any_spec] * 4,
        scratch_shapes=[
            pltpu.VMEM((HEADS, 2, 8, 5, 32, D), BF16),
            pltpu.VMEM((HEADS, 2, 4, 3, 32, D), BF16),
            pltpu.VMEM((HEADS, 2, 4, 3, 32, D), BF16),
            pltpu.VMEM((2, 2, 8, 5, 32, D), F32),
            pltpu.VMEM((HEADS, 2, 4, 3, 32, D), F32),
            pltpu.VMEM((HEADS, 2, 2, 2, 4, 32, D), BF16),
            pltpu.VMEM((HEADS, 2, 2, 2, 4, 32, D), BF16),
            pltpu.VMEM((HEADS, 2, 2, 2, 3, 32, D), BF16),
            pltpu.VMEM((HEADS, 2, 2, 2, 3, 32, D), BF16),
            pltpu.VMEM((HEADS, 4, 4, 3, 32, D), BF16),
            pltpu.VMEM((3, 768, 128), F32),
            pltpu.VMEM((128, 128), BF16),
            pltpu.VMEM((128, 128), BF16),
            pltpu.SemaphoreType.DMA((HEADS, 4)),
            pltpu.SemaphoreType.DMA((HEADS, 4)),
        ]
        + [pair] * 2
        + [pltpu.SemaphoreType.DMA((HEADS, 2, 4))] * 2
        + [pltpu.SemaphoreType.DMA((HEADS, 2, 2))] * 2
        + [pair] * 2,
        compiler_params=pltpu.CompilerParams(
            collective_id=0, has_side_effects=True, vmem_limit_bytes=56 * 1024 * 1024
        ),
    )(reach_tiles, *ins)
    return tuple(x.reshape(shape) for x in outs)


def solution(mesh):
    spec = P(None, "ha", "wa", None)
    return jax.shard_map(
        functools.partial(per_device, mesh.shape["ha"], mesh.shape["wa"]),
        mesh=mesh,
        in_specs=(spec, spec, spec, spec, P("ha", "wa", None)),
        out_specs=(spec, spec, spec, spec),
        check_vma=False,
    )
```

profile of v0, /device:TPU:28, one launch (start us, length us, event | category | flops | bytes accessed | tf_op | source)
XLA Modules:
  0.0 119.5 jit_solution(497850494748667738)
XLA Ops:
  0.6 112.0 %shard_map.84 = (bf16[4,3,32,1536]{3,2,1,0:T(8,128)(2,1)}, bf16[4,3,32,1536]{3,2,1,0:T(8,128)(2,1)}, bf16[4,3,32,1536]{3,2,1,0:T(8,128)(2,1)}, bf16[4,3,32,1536]{3,2,1,0:T(8,128)(2,1)}) custom-call(s32[3,2,4]{2,1,0:T(2,128)} %reach.1, bf16[4,3,32,1536]{3,2,1,0:T(8,128)(2,1)} %bitcast.12, bf16[4,3,32,1536]{3,2,1,0:T(8,128)(2,1)} %bitcast.13, ...), custom_call_target="tpu_custom_call" | custom-call | tf_op jit(solution)/shard_map/pallas_call | solution.py:336
  112.6 0.0 copy-start.2
  112.7 2.5 %copy.13 = bf16[4,12,8,1536]{3,2,1,0:T(8,128)(2,1)} copy(bf16[4,12,8,1536]{3,2,1,0:T(8,128)(2,1)} %bitcast.11) | data formatting | bytes 2359296
  115.1 0.0 copy-done.2
  115.1 0.0 copy-start.1
  115.1 1.0 copy.14
  116.1 0.7 copy-done.1
  116.8 0.0 copy-start
  116.8 1.0 copy.15
  117.8 0.7 copy-done
  118.5 1.0 copy.16
Async XLA Ops:
  112.6 2.5 %copy-start.2 = (bf16[4,3,32,1536]{3,2,1,0:T(8,128)(2,1)S(1)}, bf16[4,3,32,1536]{3,2,1,0:T(8,128)(2,1)}, u32[]{:S(2)}) copy-start(bf16[4,3,32,1536]{3,2,1,0:T(8,128)(2,1)} %get-tuple-element.9) | copy-start | bytes 3538948
  115.1 1.7 %copy-start.1 = (bf16[4,3,32,1536]{3,2,1,0:T(8,128)(2,1)S(1)}, bf16[4,3,32,1536]{3,2,1,0:T(8,128)(2,1)}, u32[]{:S(2)}) copy-start(bf16[4,3,32,1536]{3,2,1,0:T(8,128)(2,1)} %get-tuple-element.10) | copy-start | bytes 3538948
  116.8 1.7 %copy-start = (bf16[4,3,32,1536]{3,2,1,0:T(8,128)(2,1)S(1)}, bf16[4,3,32,1536]{3,2,1,0:T(8,128)(2,1)}, u32[]{:S(2)}) copy-start(bf16[4,3,32,1536]{3,2,1,0:T(8,128)(2,1)} %get-tuple-element.11) | copy-start | bytes 3538948
where the time goes:
time: 122 us; the launch traced here: 120 us
  Pallas kernels  112 us (92%)
  local copies, waits for them, and re-layouts  6.86 us (6%)
    pallas_call x1, Pallas kernels, per_device(): pl.pallas_call(functools.partial(kernel, size_a, size_w), out_shape=[jax....  112 us
    unnamed x10, local copies, waits for them, and re-layouts  6.86 us

commit v1 on v0

--- a/solution.py
+++ b/solution.py
@@ -14,6 +14,7 @@
 MESH = pl.DeviceIdType.MESH
 AHEAD = 4
 CORNERS_AHEAD = 2
+BEHIND = 4
 NEGATIVE = -1e30
 SCALE = 1.0 / math.sqrt(D)
 LOG2E = 1.4426950408889634
@@ -28,8 +29,8 @@
 
 def kernel(
     size_a, size_w, reach, q_in, k_in, v_in, g_in, o_out, dq_out, dk_out, dv_out,
-    kall, qg, pack, acc, own, g3s, g3r, g4s, g4r, ob, bias, perm, perm_t,
-    in_sem, out_sem, ss1, rs1, ss2, rs2, ss3, rs3, ss4, rs4,
+    kall, qg, pack, acc, own, g3s, g3r, g4s, g4r, bias, perm, perm_t,
+    in_sem, ss1, rs1, ss2, rs2, ss3, rs3, ss4, rs4,
 ):
     half_a = size_a // 2
     ia = lax.axis_index("ha")
@@ -49,10 +50,6 @@
         src = (k_in, v_in, q_in, g_in)[n].at[:, :, :, lanes(h)]
         dst = kall.at[h, n, 2:6, 1:4] if n < 2 else qg.at[h, n - 2]
         return pltpu.make_async_copy(src, dst, in_sem.at[h, n])
-
-    def store(h, n):
-        dst = (o_out, dq_out, dk_out, dv_out)[n].at[:, :, :, lanes(h)]
-        return pltpu.make_async_copy(ob.at[h, n], dst, out_sem.at[h, n])
 
     def remote(src, dst, ss, rs, dev):
         return pltpu.make_async_remote_copy(
@@ -214,8 +211,8 @@
         send_rows(h, (0, 3))
 
     def attend(h, slot, a):
-        kk = kall[h, 0, :, pl.ds(a, 3)].reshape(768, D)
-        vv = kall[h, 1, :, pl.ds(a, 3)].reshape(768, D)
+        kk = kall[h, 0, :, a : a + 3].reshape(768, D)
+        vv = kall[h, 1, :, a : a + 3].reshape(768, D)
         q = qg[h, 0, :, a].reshape(128, D)
         g = qg[h, 1, :, a].reshape(128, D)
         s = dot(kk, q, 1, 1) * (SCALE * LOG2E) + bias[a]
@@ -225,10 +222,10 @@
         dp = dot(vv, g, 1, 1)
         delta = jnp.sum(p * dp, axis=0, keepdims=True)
         ds = (p * (dp - delta)).astype(BF16)
-        ob[h, 0, :, a] = dot(low, vv, 0, 0).astype(BF16).reshape(4, 32, D)
-        ob[h, 1, :, a] = (dot(ds, kk, 0, 0) * SCALE).astype(BF16).reshape(4, 32, D)
-        acc[slot, 0, :, pl.ds(a, 3)] += dot(ds, q, 1, 0).reshape(8, 3, 32, D)
-        acc[slot, 1, :, pl.ds(a, 3)] += dot(low, g, 1, 0).reshape(8, 3, 32, D)
+        o_out[:, a, :, lanes(h)] = dot(low, vv, 0, 0).astype(BF16).reshape(4, 32, D)
+        dq_out[:, a, :, lanes(h)] = (dot(ds, kk, 0, 0) * SCALE).astype(BF16).reshape(4, 32, D)
+        acc[slot, 0, :, a : a + 3] += dot(ds, q, 1, 0).reshape(8, 3, 32, D)
+        acc[slot, 1, :, a : a + 3] += dot(low, g, 1, 0).reshape(8, 3, 32, D)
 
     def reduce_rows(h, slot):
         for s, row in ((0, 1), (1, 3)):
@@ -248,46 +245,6 @@
         send(grad_col_copy, h, sides)
         own[h] = acc[slot, :, 2:6, 1:4]
 
-    for h in range(CORNERS_AHEAD):
-        forward(h)
-
-    def step(h):
-        slot = h % 2
-
-        @pl.when(h + CORNERS_AHEAD < HEADS)
-        def _():
-            forward(h + CORNERS_AHEAD)
-
-        @pl.when(h + AHEAD < HEADS)
-        def _():
-            send_edges(h + AHEAD)
-
-        load(h, 2).wait()
-        load(h, 3).wait()
-        for s in range(2):
-            for j in range(4):
-                receive_row(h, s, j)
-        acc[slot] = jnp.zeros((2, 8, 5, 32, D), F32)
-        lax.fori_loop(0, 3, lambda a, c: (attend(h, slot, a), c)[1], 0)
-        store(h, 0).start()
-        store(h, 1).start()
-        for s in range(2):
-            for half in range(2):
-                g3s[h, s, half] = acc[slot, :, 4 * half : 4 * half + 4, 4 * s].astype(BF16)
-
-            @pl.when(ends[s][0])
-            def _():
-                for half in range(2):
-                    grad_row_copy(h, s, half).start()
-
-
-        @pl.when(h >= 1)
-        def _():
-            reduce_rows(h - 1, 1 - slot)
-
-    loop(step)
-    reduce_rows(HEADS - 1, (HEADS - 1) % 2)
-
     def finish(h):
         for s in range(2):
             receive(grad_col_copy, h, sides, s)
@@ -297,15 +254,55 @@
                 y = dot(perm[...], x, 1, 0) + own[h, kv, :, a].reshape(128, D)
                 if kv == 0:
                     y = y * SCALE
-                ob[h, 2 + kv, :, a] = y.astype(BF16).reshape(4, 32, D)
-        store(h, 2).start()
-        store(h, 3).start()
-
-    loop(finish)
+                (dk_out, dv_out)[kv][:, a, :, lanes(h)] = y.astype(BF16).reshape(4, 32, D)
+
+    for h in range(CORNERS_AHEAD):
+        forward(h)
+
+    def step(h):
+        slot = h % 2
+
+        @pl.when(h + CORNERS_AHEAD < HEADS)
+        def _():
+            forward(h + CORNERS_AHEAD)
+
+        @pl.when(h + AHEAD < HEADS)
+        def _():
+            send_edges(h + AHEAD)
+
+        load(h, 2).wait()
+        load(h, 3).wait()
+        for s in range(2):
+            for j in range(4):
+                receive_row(h, s, j)
+        acc[slot] = jnp.zeros((2, 8, 5, 32, D), F32)
+        for a in range(3):
+            attend(h, slot, a)
+        for s in range(2):
+            for half in range(2):
+                g3s[h, s, half] = acc[slot, :, 4 * half : 4 * half + 4, 4 * s].astype(BF16)
+
+            @pl.when(ends[s][0])
+            def _():
+                for half in range(2):
+                    grad_row_copy(h, s, half).start()
+
+
+        @pl.when(h >= 1)
+        def _():
+            reduce_rows(h - 1, 1 - slot)
+
+        @pl.when(h >= BEHIND)
+        def _():
+            finish(h - BEHIND)
+
+    loop(step)
+    reduce_rows(HEADS - 1, (HEADS - 1) % 2)
+
+    for h in range(HEADS - BEHIND, HEADS):
+        finish(h)
 
     def drain(h):
-        for n in range(4):
-            store(h, n).wait()
         for copy in (col_copy, grad_col_copy):
             for s, (there, dev) in enumerate(sides):
 
@@ -328,16 +325,26 @@
     loop(drain)
 
 
+def write_out(*refs):
+    sources, outs, sem = refs[:4], refs[4:8], refs[8]
+    copies = [pltpu.make_async_copy(x.at[f], y.at[f], sem.at[n, f]) for n, (x, y) in enumerate(zip(sources, outs)) for f in range(4)]
+    for copy in copies:
+        copy.start()
+    for copy in copies:
+        copy.wait()
+
+
 def per_device(size_a, size_w, queries, key_heads, value_heads, out_grad, reach_tiles):
     shape = queries.shape
     ins = [x.reshape(4, 3, 32, HEADS * D) for x in (queries, key_heads, value_heads, out_grad)]
+    ins = [pltpu.with_memory_space_constraint(x, pltpu.HBM) for x in ins]
     any_spec = pl.BlockSpec(memory_space=pl.ANY)
     pair = pltpu.SemaphoreType.DMA((HEADS, 2))
-    outs = pl.pallas_call(
+    results = pl.pallas_call(
         functools.partial(kernel, size_a, size_w),
-        out_shape=[jax.ShapeDtypeStruct((4, 3, 32, HEADS * D), BF16)] * 4,
+        out_shape=[pltpu.VMEM((4, 3, 32, HEADS * D), BF16)] * 4,
         in_specs=[pl.BlockSpec(memory_space=pltpu.SMEM)] + [any_spec] * 4,
-        out_specs=[any_spec] * 4,
+        out_specs=[pl.BlockSpec(memory_space=pltpu.VMEM)] * 4,
         scratch_shapes=[
             pltpu.VMEM((HEADS, 2, 8, 5, 32, D), BF16),
             pltpu.VMEM((HEADS, 2, 4, 3, 32, D), BF16),
@@ -348,11 +355,9 @@
             pltpu.VMEM((HEADS, 2, 2, 2, 4, 32, D), BF16),
             pltpu.VMEM((HEADS, 2, 2, 2, 3, 32, D), BF16),
             pltpu.VMEM((HEADS, 2, 2, 2, 3, 32, D), BF16),
-            pltpu.VMEM((HEADS, 4, 4, 3, 32, D), BF16),
             pltpu.VMEM((3, 768, 128), F32),
             pltpu.VMEM((128, 128), BF16),
             pltpu.VMEM((128, 128), BF16),
-            pltpu.SemaphoreType.DMA((HEADS, 4)),
             pltpu.SemaphoreType.DMA((HEADS, 4)),
         ]
         + [pair] * 2
@@ -363,6 +368,14 @@
             collective_id=0, has_side_effects=True, vmem_limit_bytes=56 * 1024 * 1024
         ),
     )(reach_tiles, *ins)
+    outs = pl.pallas_call(
+        write_out,
+        out_shape=[jax.ShapeDtypeStruct((4, 3, 32, HEADS * D), BF16)] * 4,
+        in_specs=[pl.BlockSpec(memory_space=pltpu.VMEM)] * 4,
+        out_specs=[any_spec] * 4,
+        scratch_shapes=[pltpu.SemaphoreType.DMA((4, 4))],
+        compiler_params=pltpu.CompilerParams(vmem_limit_bytes=8 * 1024 * 1024),
+    )(*(pltpu.with_memory_space_constraint(x, pltpu.VMEM) for x in results))
     return tuple(x.reshape(shape) for x in outs)
 
 

time: 122 us -> 117 us (0.959)
  the two profiles are of different devices: /device:TPU:28 before, /device:TPU:25 now
where the time goes in v1:
time: 117 us; the launch traced here: 116 us
  Pallas kernels  116 us (99%)
    pallas_call x1, Pallas kernels, per_device(): pl.pallas_call(functools.partial(kernel, size_a, size_w), out_shape=[pltp...  114 us

profile of v1, /device:TPU:25, one launch (start us, length us, event | category | flops | bytes accessed | tf_op | source)
XLA Modules:
  0.0 116.5 jit_solution(17983403058006175613)
XLA Ops:
  0.6 113.5 %shard_map.84 = (bf16[4,3,32,1536]{3,2,1,0:T(8,128)(2,1)S(1)}, bf16[4,3,32,1536]{3,2,1,0:T(8,128)(2,1)S(1)}, bf16[4,3,32,1536]{3,2,1,0:T(8,128)(2,1)S(1)}, bf16[4,3,32,1536]{3,2,1,0:T(8,128)(2,1)S(1)}) custom-call(s32[3,2,4]{2,1,0:T(2,128)} %reach.1, bf16[4,3,32,1536]{3,2,1,0:T(8,128)(2,1)} %bitcast.8, bf16[4,3,32,1536]{3,2,1,0:T(8,128)(2,1)} %bitcast.9, ...), custom_call_target="tpu_custom_call" | custom-call | tf_op jit(solution)/shard_map/pallas_call | solution.py:343
  114.2 2.3 %shard_map.85 = (bf16[4,3,32,1536]{3,2,1,0:T(8,128)(2,1)}, bf16[4,3,32,1536]{3,2,1,0:T(8,128)(2,1)}, bf16[4,3,32,1536]{3,2,1,0:T(8,128)(2,1)}, bf16[4,3,32,1536]{3,2,1,0:T(8,128)(2,1)}) custom-call(bf16[4,3,32,1536]{3,2,1,0:T(8,128)(2,1)S(1)} %get-tuple-element.12.refs_0_, bf16[4,3,32,1536]{3,2,1,0:T(8,128)(2,1)S(1)} %get-tuple-element.13.refs_1_, ...), custom_call_target="tpu_custom_call" | custom-call | tf_op jit(solution)/shard_map/pallas_call | solution.py:371

commit v2 on v1

--- a/solution.py
+++ b/solution.py
@@ -12,9 +12,13 @@
 TS = 4
 D = 128
 MESH = pl.DeviceIdType.MESH
-AHEAD = 4
-CORNERS_AHEAD = 2
-BEHIND = 4
+AHEAD = 7
+RELAY_AHEAD = 5
+CORNERS_AHEAD = 3
+ROWS_BEHIND = 2
+RELAY_BEHIND = 4
+BEHIND = 6
+SLOTS = ROWS_BEHIND + 1
 NEGATIVE = -1e30
 SCALE = 1.0 / math.sqrt(D)
 LOG2E = 1.4426950408889634
@@ -29,8 +33,8 @@
 
 def kernel(
     size_a, size_w, reach, q_in, k_in, v_in, g_in, o_out, dq_out, dk_out, dv_out,
-    kall, qg, pack, acc, own, g3s, g3r, g4s, g4r, bias, perm, perm_t,
-    in_sem, ss1, rs1, ss2, rs2, ss3, rs3, ss4, rs4,
+    kall, k_own, v_own, q_own, g_own, pack, acc, own, g3s, g3r, g4s, g4r, r1, r4, bias, perm, perm_t,
+    in_sem, ss1, rs1, ss2, rs2, ss3, rs3, ss4, rs4, ri1, ro1, ri4, ro4,
 ):
     half_a = size_a // 2
     ia = lax.axis_index("ha")
@@ -43,13 +47,29 @@
     ends = ((has_u, up), (has_d, down))
     crossed = (ia == half_a, ia == half_a - 1)
 
+    parity, ring, rings = iw % 2, iw // 2, size_w // 2
+    out = 2 * parity - 1
+    shared = jnp.where(parity == 1, ring + 1, rings - ring)
+    carried = jnp.where(parity == 1, ring, rings - 1 - ring)
+    middle = (ia >= half_a - 2) & (ia < half_a + 2)
+
+    def chosen(k, part, fewer):
+        n = part * HEADS // rings - jnp.where(middle & (part > 0), fewer, 0)
+        return (k * n) % HEADS >= HEADS - n
+
+    def relayed_col(h, part):
+        return chosen(h, part, jnp.where(part >= 2, 1, 0))
+
+    def relayed_grad(h, part):
+        return chosen(HEADS - 1 - h, part, jnp.where(part >= 3, 2, 1))
+
     def lanes(h):
         return pl.ds(pl.multiple_of(h * D, D), D)
 
-    def load(h, n):
-        src = (k_in, v_in, q_in, g_in)[n].at[:, :, :, lanes(h)]
-        dst = kall.at[h, n, 2:6, 1:4] if n < 2 else qg.at[h, n - 2]
-        return pltpu.make_async_copy(src, dst, in_sem.at[h, n])
+    loads = [
+        pltpu.make_async_copy(src, dst, in_sem.at[n])
+        for n, (src, dst) in enumerate(((k_in, k_own), (v_in, v_own), (q_in, q_own), (g_in, g_own)))
+    ]
 
     def remote(src, dst, ss, rs, dev):
         return pltpu.make_async_remote_copy(
@@ -98,15 +118,45 @@
             g3s.at[h, s, half], g3r.at[h, 1 - s, to], ss3.at[h, s, half], rs3.at[h, 1 - s, to], (ia + (2 * s - 1), col)
         )
 
+    def col_relay_in(h, s):
+        return remote(pack.at[h, :, 2 * s : 2 * s + 2], r1.at[h], ss1.at[h, s], ri1.at[h], (ia, iw + 2 * out))
+
+    def col_relay_out(h):
+        dst = kall.at[h, :, pl.ds(6 - 6 * parity, 2), 1:4]
+        return remote(r1.at[h], dst, ro1.at[h], rs1.at[h, 1 - parity], (ia, iw - out))
+
+    def grad_relay_in(h, s):
+        return remote(g4s.at[h, s], r4.at[h], ss4.at[h, s], ri4.at[h], (ia, iw + 2 * out))
+
+    def grad_relay_out(h):
+        return remote(r4.at[h], g4r.at[h, 1 - parity], ro4.at[h], rs4.at[h, 1 - parity], (ia, iw - out))
+
     def grad_col_copy(h, s, dev):
         return remote(g4s.at[h, s], g4r.at[h, 1 - s], ss4.at[h, s], rs4.at[h, 1 - s], dev)
 
-    def send(copy, h, group):
-        for s, (there, dev) in enumerate(group):
-
-            @pl.when(there)
+    def send(direct, by_relay, relayed, h):
+        for s, (there, dev) in enumerate(sides):
+            through = (parity == s) & relayed(h, shared)
+
+            @pl.when(there & through)
             def _():
-                copy(h, s, dev).start()
+                by_relay(h, s).start()
+
+            @pl.when(there & jnp.logical_not(through))
+            def _():
+                direct(h, s, dev).start()
+
+    def relay_col(h):
+        @pl.when(relayed_col(h, carried))
+        def _():
+            remote(r1.at[h], r1.at[h], ro1.at[h], ri1.at[h], (ia, iw - out)).wait_recv()
+            col_relay_out(h).start()
+
+    def relay_grad(h):
+        @pl.when(relayed_grad(h, carried))
+        def _():
+            remote(r4.at[h], r4.at[h], ro4.at[h], ri4.at[h], (ia, iw - out)).wait_recv()
+            grad_relay_out(h).start()
 
     def receive(copy, h, group, s):
         there, dev = group[s]
@@ -118,21 +168,14 @@
     def loop(body):
         lax.fori_loop(0, HEADS, lambda h, c: (body(h), c)[1], 0)
 
-    def load_kv(h):
-        load(h, 0).start()
-        load(h, 1).start()
-
-    def load_qg(h):
-        load(h, 2).start()
-        load(h, 3).start()
-
-    loop(load_kv)
-    loop(load_qg)
+    for load in loads:
+        load.start()
 
     barrier = pltpu.get_barrier_semaphore()
     greeted = sides + ends
     for s, row in ((0, ia - 1), (1, ia + 1)):
         greeted += ((crossed[s] & has_l, (row, iw - 1)), (crossed[s] & has_r, (row, iw + 1)))
+    greeted += ((iw >= 2, (ia, iw - 2)), (iw < size_w - 2, (ia, iw + 2)))
     for there, dev in greeted:
 
         @pl.when(there)
@@ -169,17 +212,20 @@
     count = sum(there.astype(jnp.int32) for there, _ in greeted)
     pl.semaphore_wait(barrier, count)
 
+    loads[0].wait()
+    loads[1].wait()
+
     def send_edges(h):
-        load(h, 0).wait()
-        load(h, 1).wait()
         for kv in range(2):
             for a in range(3):
-                x = kall[h, kv, 2:6, a + 1].reshape(128, D)
+                x = (k_own, v_own)[kv][:, a, :, lanes(h)]
+                kall[h, kv, 2:6, a + 1] = x
+                x = x.reshape(128, D)
                 pack[h, kv, :, a] = dot(perm_t[...], x, 1, 0).astype(BF16).reshape(4, 32, D)
         send_rows(h, (1, 2))
-        send(col_copy, h, sides)
-
-    for h in range(AHEAD):
+        send(col_copy, col_relay_in, relayed_col, h)
+
+    for h in range(3):
         send_edges(h)
 
     shape = (8, 3, 32, 128)
@@ -213,8 +259,8 @@
     def attend(h, slot, a):
         kk = kall[h, 0, :, a : a + 3].reshape(768, D)
         vv = kall[h, 1, :, a : a + 3].reshape(768, D)
-        q = qg[h, 0, :, a].reshape(128, D)
-        g = qg[h, 1, :, a].reshape(128, D)
+        q = q_own[:, a, :, lanes(h)].reshape(128, D)
+        g = g_own[:, a, :, lanes(h)].reshape(128, D)
         s = dot(kk, q, 1, 1) * (SCALE * LOG2E) + bias[a]
         p = jnp.exp2(s - jnp.max(s, axis=0, keepdims=True))
         p = p * (1.0 / jnp.sum(p, axis=0, keepdims=True))
@@ -242,7 +288,7 @@
 
         for s in range(2):
             g4s[h, s] = acc[slot, :, 6 * s : 6 * s + 2, 1:4].astype(BF16)
-        send(grad_col_copy, h, sides)
+        send(grad_col_copy, grad_relay_in, relayed_grad, h)
         own[h] = acc[slot, :, 2:6, 1:4]
 
     def finish(h):
@@ -256,22 +302,31 @@
                     y = y * SCALE
                 (dk_out, dv_out)[kv][:, a, :, lanes(h)] = y.astype(BF16).reshape(4, 32, D)
 
-    for h in range(CORNERS_AHEAD):
-        forward(h)
+    for h in range(RELAY_AHEAD):
+        relay_col(h)
+        if h < CORNERS_AHEAD:
+            forward(h)
+        if h + 3 < AHEAD:
+            send_edges(h + 3)
+
+    loads[2].wait()
+    loads[3].wait()
 
     def step(h):
-        slot = h % 2
+        slot = h % SLOTS
 
         @pl.when(h + CORNERS_AHEAD < HEADS)
         def _():
             forward(h + CORNERS_AHEAD)
 
+        @pl.when(h + RELAY_AHEAD < HEADS)
+        def _():
+            relay_col(h + RELAY_AHEAD)
+
         @pl.when(h + AHEAD < HEADS)
         def _():
             send_edges(h + AHEAD)
 
-        load(h, 2).wait()
-        load(h, 3).wait()
         for s in range(2):
             for j in range(4):
                 receive_row(h, s, j)
@@ -288,21 +343,36 @@
                     grad_row_copy(h, s, half).start()
 
 
-        @pl.when(h >= 1)
-        def _():
-            reduce_rows(h - 1, 1 - slot)
+        @pl.when(h >= ROWS_BEHIND)
+        def _():
+            reduce_rows(h - ROWS_BEHIND, (h - ROWS_BEHIND) % SLOTS)
+
+        @pl.when(h >= RELAY_BEHIND)
+        def _():
+            relay_grad(h - RELAY_BEHIND)
 
         @pl.when(h >= BEHIND)
         def _():
             finish(h - BEHIND)
 
     loop(step)
-    reduce_rows(HEADS - 1, (HEADS - 1) % 2)
-
+    for h in range(HEADS - ROWS_BEHIND, HEADS):
+        reduce_rows(h, h % SLOTS)
+
+    for h in range(HEADS - RELAY_BEHIND, HEADS):
+        relay_grad(h)
     for h in range(HEADS - BEHIND, HEADS):
         finish(h)
 
     def drain(h):
+        @pl.when(relayed_col(h, carried))
+        def _():
+            col_relay_out(h).wait_send()
+
+        @pl.when(relayed_grad(h, carried))
+        def _():
+            grad_relay_out(h).wait_send()
+
         for copy in (col_copy, grad_col_copy):
             for s, (there, dev) in enumerate(sides):
 
@@ -347,23 +417,29 @@
         out_specs=[pl.BlockSpec(memory_space=pltpu.VMEM)] * 4,
         scratch_shapes=[
             pltpu.VMEM((HEADS, 2, 8, 5, 32, D), BF16),
+            pltpu.VMEM((4, 3, 32, HEADS * D), BF16),
+            pltpu.VMEM((4, 3, 32, HEADS * D), BF16),
+            pltpu.VMEM((4, 3, 32, HEADS * D), BF16),
+            pltpu.VMEM((4, 3, 32, HEADS * D), BF16),
             pltpu.VMEM((HEADS, 2, 4, 3, 32, D), BF16),
-            pltpu.VMEM((HEADS, 2, 4, 3, 32, D), BF16),
-            pltpu.VMEM((2, 2, 8, 5, 32, D), F32),
+            pltpu.VMEM((SLOTS, 2, 8, 5, 32, D), F32),
             pltpu.VMEM((HEADS, 2, 4, 3, 32, D), F32),
             pltpu.VMEM((HEADS, 2, 2, 2, 4, 32, D), BF16),
             pltpu.VMEM((HEADS, 2, 2, 2, 4, 32, D), BF16),
             pltpu.VMEM((HEADS, 2, 2, 2, 3, 32, D), BF16),
             pltpu.VMEM((HEADS, 2, 2, 2, 3, 32, D), BF16),
+            pltpu.VMEM((HEADS, 2, 2, 3, 32, D), BF16),
+            pltpu.VMEM((HEADS, 2, 2, 3, 32, D), BF16),
             pltpu.VMEM((3, 768, 128), F32),
             pltpu.VMEM((128, 128), BF16),
             pltpu.VMEM((128, 128), BF16),
-            pltpu.SemaphoreType.DMA((HEADS, 4)),
+            pltpu.SemaphoreType.DMA((4,)),
         ]
         + [pair] * 2
         + [pltpu.SemaphoreType.DMA((HEADS, 2, 4))] * 2
         + [pltpu.SemaphoreType.DMA((HEADS, 2, 2))] * 2
-        + [pair] * 2,
+        + [pair] * 2
+        + [pltpu.SemaphoreType.DMA((HEADS,))] * 4,
         compiler_params=pltpu.CompilerParams(
             collective_id=0, has_side_effects=True, vmem_limit_bytes=56 * 1024 * 1024
         ),

time: 117 us -> 112 us (0.957)
  the two profiles are of different devices: /device:TPU:25 before, /device:TPU:28 now
where the time goes in v2:
time: 112 us; the launch traced here: 111 us
  Pallas kernels  111 us (99%)
    pallas_call x1, Pallas kernels, per_device(): pl.pallas_call(functools.partial(kernel, size_a, size_w), out_shape=[pltp...  109 us
    pallas_call x1, Pallas kernels, per_device(): pl.pallas_call(write_out, out_shape=[jax.ShapeDtypeStruct((4, 3, 32, HEAD...  2.31 us

profile of v2, /device:TPU:28, one launch (start us, length us, event | category | flops | bytes accessed | tf_op | source)
XLA Modules:
  0.0 111.5 jit_solution(2829485786303322071)
XLA Ops:
  0.6 108.5 %shard_map.84 = (bf16[4,3,32,1536]{3,2,1,0:T(8,128)(2,1)S(1)}, bf16[4,3,32,1536]{3,2,1,0:T(8,128)(2,1)S(1)}, bf16[4,3,32,1536]{3,2,1,0:T(8,128)(2,1)S(1)}, bf16[4,3,32,1536]{3,2,1,0:T(8,128)(2,1)S(1)}) custom-call(s32[3,2,4]{2,1,0:T(2,128)} %reach.1, bf16[4,3,32,1536]{3,2,1,0:T(8,128)(2,1)} %bitcast.8, bf16[4,3,32,1536]{3,2,1,0:T(8,128)(2,1)} %bitcast.9, ...), custom_call_target="tpu_custom_call" | custom-call | tf_op jit(solution)/shard_map/pallas_call | solution.py:413
  109.2 2.3 %shard_map.85 = (bf16[4,3,32,1536]{3,2,1,0:T(8,128)(2,1)}, bf16[4,3,32,1536]{3,2,1,0:T(8,128)(2,1)}, bf16[4,3,32,1536]{3,2,1,0:T(8,128)(2,1)}, bf16[4,3,32,1536]{3,2,1,0:T(8,128)(2,1)}) custom-call(bf16[4,3,32,1536]{3,2,1,0:T(8,128)(2,1)S(1)} %get-tuple-element.12.refs_0_, bf16[4,3,32,1536]{3,2,1,0:T(8,128)(2,1)S(1)} %get-tuple-element.13.refs_1_, ...), custom_call_target="tpu_custom_call" | custom-call | tf_op jit(solution)/shard_map/pallas_call | solution.py:447

commit v3 on v2

--- a/solution.py
+++ b/solution.py
@@ -18,7 +18,6 @@
 ROWS_BEHIND = 2
 RELAY_BEHIND = 4
 BEHIND = 6
-SLOTS = ROWS_BEHIND + 1
 NEGATIVE = -1e30
 SCALE = 1.0 / math.sqrt(D)
 LOG2E = 1.4426950408889634
@@ -33,7 +32,7 @@
 
 def kernel(
     size_a, size_w, reach, q_in, k_in, v_in, g_in, o_out, dq_out, dk_out, dv_out,
-    kall, k_own, v_own, q_own, g_own, pack, acc, own, g3s, g3r, g4s, g4r, r1, r4, bias, perm, perm_t,
+    kall, k_own, v_own, q_own, g_own, pack, acc, g3s, g3r, g4s, g4r, r1, r4, bias, perm, perm_t,
     in_sem, ss1, rs1, ss2, rs2, ss3, rs3, ss4, rs4, ri1, ro1, ri4, ro4,
 ):
     half_a = size_a // 2
@@ -212,23 +211,28 @@
     count = sum(there.astype(jnp.int32) for there, _ in greeted)
     pl.semaphore_wait(barrier, count)
 
+    def permute(matrix, x, y):
+        z = dot(matrix[...], jnp.concatenate([x, y], axis=1), 1, 0)
+        return z[:, :D], z[:, D:]
+
     loads[0].wait()
     loads[1].wait()
 
     def send_edges(h):
-        for kv in range(2):
-            for a in range(3):
-                x = (k_own, v_own)[kv][:, a, :, lanes(h)]
-                kall[h, kv, 2:6, a + 1] = x
-                x = x.reshape(128, D)
-                pack[h, kv, :, a] = dot(perm_t[...], x, 1, 0).astype(BF16).reshape(4, 32, D)
+        for a in range(3):
+            x = [own[:, a, :, lanes(h)] for own in (k_own, v_own)]
+            kall[h, 0, 2:6, a + 1] = x[0]
+            kall[h, 1, 2:6, a + 1] = x[1]
+            y = permute(perm_t, x[0].reshape(128, D), x[1].reshape(128, D))
+            pack[h, 0, :, a] = y[0].astype(BF16).reshape(4, 32, D)
+            pack[h, 1, :, a] = y[1].astype(BF16).reshape(4, 32, D)
         send_rows(h, (1, 2))
         send(col_copy, col_relay_in, relayed_col, h)
 
     for h in range(3):
         send_edges(h)
 
-    shape = (8, 3, 32, 128)
+    shape = (6, 3, 32, 128)
     unit = lax.broadcasted_iota(jnp.int32, shape, 0)
     drow = lax.broadcasted_iota(jnp.int32, shape, 1) - 1
     token = lax.broadcasted_iota(jnp.int32, shape, 2)
@@ -237,8 +241,8 @@
     for a in range(3):
         own_col = (token >> 2) & 1
         if a != 1:
-            own_col = jnp.where(drow == a - 1, (unit >> 1) - 1, own_col)
-        kcol = jnp.where((unit >= 2) & (unit < 6), own_col, (unit >> 1) - 1)
+            own_col = jnp.where(drow == a - 1, unit >> 1, own_col)
+        kcol = jnp.where(unit < 4, own_col, 3 * qcol - 1)
         dcol = kcol - qcol
         acol = iw * 2 + kcol
         in_cols = (acol >= 0) & (acol < 2 * size_w)
@@ -249,58 +253,104 @@
         arow = ia * 3 + a + drow
         ok = in_cols & (arow >= 0) & (arow < 3 * size_a)
         ok = ok & (drow >= -of(0)) & (drow <= of(1)) & (dcol >= -of(2)) & (dcol <= of(3))
-        bias[a] = jnp.where(ok, 0.0, NEGATIVE).astype(F32).reshape(768, 128)
+        bias[a] = jnp.where(ok, 0.0, NEGATIVE).astype(F32).reshape(576, 128)
 
     def forward(h):
         receive(col_copy, h, sides, 0)
         receive(col_copy, h, sides, 1)
         send_rows(h, (0, 3))
 
-    def attend(h, slot, a):
-        kk = kall[h, 0, :, a : a + 3].reshape(768, D)
-        vv = kall[h, 1, :, a : a + 3].reshape(768, D)
+    left_query = ((lax.broadcasted_iota(jnp.int32, (128, D), 0) >> 2) & 1) == 0
+    none = jnp.zeros((128, D), BF16)
+
+    def attend(h, a):
+        def keys(kv, lo, hi):
+            return kall[h, kv, lo:hi, a : a + 3].reshape((hi - lo) * 96, D)
+
+        def halo(kv):
+            return jnp.concatenate([keys(kv, 0, 2), keys(kv, 6, 8)], axis=1)
+
+        def by_side(x):
+            return jnp.concatenate([jnp.where(left_query, x, none), jnp.where(left_query, none, x)], axis=1)
+
+        def own_side(x):
+            return jnp.where(left_query, x[:, :D], x[:, D:])
+
+        k_mid, v_mid, k_halo, v_halo = keys(0, 2, 6), keys(1, 2, 6), halo(0), halo(1)
         q = q_own[:, a, :, lanes(h)].reshape(128, D)
         g = g_own[:, a, :, lanes(h)].reshape(128, D)
-        s = dot(kk, q, 1, 1) * (SCALE * LOG2E) + bias[a]
+        both = jnp.concatenate([jnp.concatenate([q, none], axis=1), jnp.concatenate([none, g], axis=1)], axis=0)
+        q_side, g_side = by_side(q), by_side(g)
+        mid = dot(jnp.concatenate([k_mid, v_mid], axis=1), both, 1, 1)
+        s = jnp.concatenate([mid[:, :128], dot(k_halo, q_side, 1, 1)], axis=0)
+        dp = jnp.concatenate([mid[:, 128:], dot(v_halo, g_side, 1, 1)], axis=0)
+        s = s * (SCALE * LOG2E) + bias[a]
         p = jnp.exp2(s - jnp.max(s, axis=0, keepdims=True))
         p = p * (1.0 / jnp.sum(p, axis=0, keepdims=True))
         low = p.astype(BF16)
-        dp = dot(vv, g, 1, 1)
-        delta = jnp.sum(p * dp, axis=0, keepdims=True)
-        ds = (p * (dp - delta)).astype(BF16)
-        o_out[:, a, :, lanes(h)] = dot(low, vv, 0, 0).astype(BF16).reshape(4, 32, D)
-        dq_out[:, a, :, lanes(h)] = (dot(ds, kk, 0, 0) * SCALE).astype(BF16).reshape(4, 32, D)
-        acc[slot, 0, :, a : a + 3] += dot(ds, q, 1, 0).reshape(8, 3, 32, D)
-        acc[slot, 1, :, a : a + 3] += dot(low, g, 1, 0).reshape(8, 3, 32, D)
-
-    def reduce_rows(h, slot):
-        for s, row in ((0, 1), (1, 3)):
+        t = p * dp
+        ds = (t - p * jnp.sum(t, axis=0, keepdims=True)).astype(BF16)
+        o = dot(low[:384], v_mid, 0, 0) + own_side(dot(low[384:], v_halo, 0, 0))
+        dq = dot(ds[:384], k_mid, 0, 0) + own_side(dot(ds[384:], k_halo, 0, 0))
+        o_out[:, a, :, lanes(h)] = o.astype(BF16).reshape(4, 32, D)
+        dq_out[:, a, :, lanes(h)] = (dq * SCALE).astype(BF16).reshape(4, 32, D)
+        mid = dot(jnp.concatenate([ds[:384], low[:384]], axis=1), both, 1, 0)
+        sums = ((mid[:, :D], dot(ds[384:], q_side, 1, 0)), (mid[:, D:], dot(low[384:], g_side, 1, 0)))
+        for kv, (own, beside) in enumerate(sums):
+            own = own.reshape(4, 3, 32, D)
+            two = (beside[:, :D].reshape(2, 3, 32, D), beside[:, D:].reshape(2, 3, 32, D))
+            for i in range(3):
+                row = a + i - 1
+                if row in (-1, 3):
+                    end = 0 if row < 0 else 1
+                    g3s[h, end, 0, kv, 0:2] = two[0][:, i].astype(BF16)
+                    g3s[h, end, 0, kv, 2:4] = own[0:2, i].astype(BF16)
+                    g3s[h, end, 1, kv, 0:2] = own[2:4, i].astype(BF16)
+                    g3s[h, end, 1, kv, 2:4] = two[1][:, i].astype(BF16)
+                elif row > a or a == 0:
+                    acc[h, kv, 0:2, row] = two[0][:, i]
+                    acc[h, kv, 2:6, row] = own[:, i]
+                    acc[h, kv, 6:8, row] = two[1][:, i]
+                else:
+                    acc[h, kv, 0:2, row] += two[0][:, i]
+                    acc[h, kv, 2:6, row] += own[:, i]
+                    acc[h, kv, 6:8, row] += two[1][:, i]
+
+    def send_grad_rows(h, s):
+        @pl.when(ends[s][0])
+        def _():
+            for half in range(2):
+                grad_row_copy(h, s, half).start()
+
+    def reduce_rows(h):
+        for s in range(2):
+            row = 2 * s
+
             @pl.when(ends[s][0])
             def _():
                 for half in range(2):
                     ref = g3r.at[h, s, half]
                     remote(ref, ref, ss3.at[h, s, half], rs3.at[h, s, half], ends[s][1]).wait_recv()
-                acc[slot, :, 0:2, row] += g3r[h, s, 0, :, 0:2].astype(F32)
-                acc[slot, :, 6:8, row] += g3r[h, s, 1, :, 2:4].astype(F32)
-                for kv in range(2):
-                    x = jnp.concatenate([g3r[h, s, 0, kv, 2:4], g3r[h, s, 1, kv, 0:2]]).reshape(128, D)
-                    acc[slot, kv, 2:6, row] += dot(perm[...], x, 1, 0).reshape(4, 32, D)
+                acc[h, :, 0:2, row] += g3r[h, s, 0, :, 0:2].astype(F32)
+                acc[h, :, 6:8, row] += g3r[h, s, 1, :, 2:4].astype(F32)
+                x = [jnp.concatenate([g3r[h, s, 0, kv, 2:4], g3r[h, s, 1, kv, 0:2]]).reshape(128, D) for kv in range(2)]
+                for kv, y in enumerate(permute(perm, x[0], x[1])):
+                    acc[h, kv, 2:6, row] += y.reshape(4, 32, D)
 
         for s in range(2):
-            g4s[h, s] = acc[slot, :, 6 * s : 6 * s + 2, 1:4].astype(BF16)
+            g4s[h, s] = acc[h, :, 6 * s : 6 * s + 2].astype(BF16)
         send(grad_col_copy, grad_relay_in, relayed_grad, h)
-        own[h] = acc[slot, :, 2:6, 1:4]
 
     def finish(h):
         for s in range(2):
             receive(grad_col_copy, h, sides, s)
-        for kv in range(2):
-            for a in range(3):
-                x = g4r[h, :, kv, :, a].reshape(128, D)
-                y = dot(perm[...], x, 1, 0) + own[h, kv, :, a].reshape(128, D)
-                if kv == 0:
-                    y = y * SCALE
-                (dk_out, dv_out)[kv][:, a, :, lanes(h)] = y.astype(BF16).reshape(4, 32, D)
+        for a in range(3):
+            x = [g4r[h, :, kv, :, a].reshape(128, D) for kv in range(2)]
+            y = permute(perm, x[0], x[1])
+            dk = (y[0].reshape(4, 32, D) + acc[h, 0, 2:6, a]) * SCALE
+            dv = y[1].reshape(4, 32, D) + acc[h, 1, 2:6, a]
+            dk_out[:, a, :, lanes(h)] = dk.astype(BF16)
+            dv_out[:, a, :, lanes(h)] = dv.astype(BF16)
 
     for h in range(RELAY_AHEAD):
         relay_col(h)
@@ -313,8 +363,6 @@
     loads[3].wait()
 
     def step(h):
-        slot = h % SLOTS
-
         @pl.when(h + CORNERS_AHEAD < HEADS)
         def _():
             forward(h + CORNERS_AHEAD)
@@ -327,25 +375,17 @@
         def _():
             send_edges(h + AHEAD)
 
-        for s in range(2):
-            for j in range(4):
-                receive_row(h, s, j)
-        acc[slot] = jnp.zeros((2, 8, 5, 32, D), F32)
         for a in range(3):
-            attend(h, slot, a)
-        for s in range(2):
-            for half in range(2):
-                g3s[h, s, half] = acc[slot, :, 4 * half : 4 * half + 4, 4 * s].astype(BF16)
-
-            @pl.when(ends[s][0])
-            def _():
-                for half in range(2):
-                    grad_row_copy(h, s, half).start()
-
+            if a != 1:
+                for j in range(4):
+                    receive_row(h, a // 2, j)
+            attend(h, a)
+            if a != 1:
+                send_grad_rows(h, a // 2)
 
         @pl.when(h >= ROWS_BEHIND)
         def _():
-            reduce_rows(h - ROWS_BEHIND, (h - ROWS_BEHIND) % SLOTS)
+            reduce_rows(h - ROWS_BEHIND)
 
         @pl.when(h >= RELAY_BEHIND)
         def _():
@@ -357,7 +397,7 @@
 
     loop(step)
     for h in range(HEADS - ROWS_BEHIND, HEADS):
-        reduce_rows(h, h % SLOTS)
+        reduce_rows(h)
 
     for h in range(HEADS - RELAY_BEHIND, HEADS):
         relay_grad(h)
@@ -422,15 +462,14 @@
             pltpu.VMEM((4, 3, 32, HEADS * D), BF16),
             pltpu.VMEM((4, 3, 32, HEADS * D), BF16),
             pltpu.VMEM((HEADS, 2, 4, 3, 32, D), BF16),
-            pltpu.VMEM((SLOTS, 2, 8, 5, 32, D), F32),
-            pltpu.VMEM((HEADS, 2, 4, 3, 32, D), F32),
+            pltpu.VMEM((HEADS, 2, 8, 3, 32, D), F32),
             pltpu.VMEM((HEADS, 2, 2, 2, 4, 32, D), BF16),
             pltpu.VMEM((HEADS, 2, 2, 2, 4, 32, D), BF16),
             pltpu.VMEM((HEADS, 2, 2, 2, 3, 32, D), BF16),
             pltpu.VMEM((HEADS, 2, 2, 2, 3, 32, D), BF16),
             pltpu.VMEM((HEADS, 2, 2, 3, 32, D), BF16),
             pltpu.VMEM((HEADS, 2, 2, 3, 32, D), BF16),
-            pltpu.VMEM((3, 768, 128), F32),
+            pltpu.VMEM((3, 576, 128), F32),
             pltpu.VMEM((128, 128), BF16),
             pltpu.VMEM((128, 128), BF16),
             pltpu.SemaphoreType.DMA((4,)),

time: 112 us -> 112 us (level)
  no operation moved by 1% of the time
where the time goes in v3:
time: 112 us
  Pallas kernels  111 us (99%)
    pallas_call x1, Pallas kernels, per_device(): pl.pallas_call(functools.partial(kernel, size_a, size_w), out_shape=[pltp...  109 us
    pallas_call x1, Pallas kernels, per_device(): pl.pallas_call(write_out, out_shape=[jax.ShapeDtypeStruct((4, 3, 32, HEAD...  2.31 us

profile of v3, /device:TPU:28, one launch (start us, length us, event | category | flops | bytes accessed | tf_op | source)
XLA Modules:
  0.0 112.0 jit_solution(10377625399842740879)
XLA Ops:
  0.6 109.0 %shard_map.84 = (bf16[4,3,32,1536]{3,2,1,0:T(8,128)(2,1)S(1)}, bf16[4,3,32,1536]{3,2,1,0:T(8,128)(2,1)S(1)}, bf16[4,3,32,1536]{3,2,1,0:T(8,128)(2,1)S(1)}, bf16[4,3,32,1536]{3,2,1,0:T(8,128)(2,1)S(1)}) custom-call(s32[3,2,4]{2,1,0:T(2,128)} %reach.1, bf16[4,3,32,1536]{3,2,1,0:T(8,128)(2,1)} %bitcast.8, bf16[4,3,32,1536]{3,2,1,0:T(8,128)(2,1)} %bitcast.9, ...), custom_call_target="tpu_custom_call" | custom-call | tf_op jit(solution)/shard_map/pallas_call | solution.py:453
  109.7 2.3 %shard_map.85 = (bf16[4,3,32,1536]{3,2,1,0:T(8,128)(2,1)}, bf16[4,3,32,1536]{3,2,1,0:T(8,128)(2,1)}, bf16[4,3,32,1536]{3,2,1,0:T(8,128)(2,1)}, bf16[4,3,32,1536]{3,2,1,0:T(8,128)(2,1)}) custom-call(bf16[4,3,32,1536]{3,2,1,0:T(8,128)(2,1)S(1)} %get-tuple-element.12.refs_0_, bf16[4,3,32,1536]{3,2,1,0:T(8,128)(2,1)S(1)} %get-tuple-element.13.refs_1_, ...), custom_call_target="tpu_custom_call" | custom-call | tf_op jit(solution)/shard_map/pallas_call | solution.py:486

commit v4 on v3

--- a/solution.py
+++ b/solution.py
@@ -16,7 +16,6 @@
 RELAY_AHEAD = 5
 CORNERS_AHEAD = 3
 ROWS_BEHIND = 2
-RELAY_BEHIND = 4
 BEHIND = 6
 NEGATIVE = -1e30
 SCALE = 1.0 / math.sqrt(D)
@@ -37,6 +36,7 @@
 ):
     half_a = size_a // 2
     ia = lax.axis_index("ha")
+    even = ia % 2 == 0
     iw = lax.axis_index("wa")
     has_u, has_d = ia > 0, ia < size_a - 1
     has_l, has_r = iw > 0, iw < size_w - 1
@@ -211,6 +211,22 @@
     count = sum(there.astype(jnp.int32) for there, _ in greeted)
     pl.semaphore_wait(barrier, count)
 
+    def send_cols(h):
+        send(col_copy, col_relay_in, relayed_col, h)
+
+    def begin(h):
+        pack_edges(h)
+
+        @pl.when(even)
+        def _():
+            send_cols(h)
+
+        send_rows(h, (1, 2))
+
+        @pl.when(jnp.logical_not(even))
+        def _():
+            send_cols(h)
+
     def permute(matrix, x, y):
         z = dot(matrix[...], jnp.concatenate([x, y], axis=1), 1, 0)
         return z[:, :D], z[:, D:]
@@ -218,7 +234,7 @@
     loads[0].wait()
     loads[1].wait()
 
-    def send_edges(h):
+    def pack_edges(h):
         for a in range(3):
             x = [own[:, a, :, lanes(h)] for own in (k_own, v_own)]
             kall[h, 0, 2:6, a + 1] = x[0]
@@ -226,11 +242,9 @@
             y = permute(perm_t, x[0].reshape(128, D), x[1].reshape(128, D))
             pack[h, 0, :, a] = y[0].astype(BF16).reshape(4, 32, D)
             pack[h, 1, :, a] = y[1].astype(BF16).reshape(4, 32, D)
-        send_rows(h, (1, 2))
-        send(col_copy, col_relay_in, relayed_col, h)
 
     for h in range(3):
-        send_edges(h)
+        begin(h)
 
     shape = (6, 3, 32, 128)
     unit = lax.broadcasted_iota(jnp.int32, shape, 0)
@@ -357,23 +371,44 @@
         if h < CORNERS_AHEAD:
             forward(h)
         if h + 3 < AHEAD:
-            send_edges(h + 3)
+            begin(h + 3)
 
     loads[2].wait()
     loads[3].wait()
 
+    def columns(h, behind):
+        @pl.when(h + RELAY_AHEAD < HEADS)
+        def _():
+            relay_col(h + RELAY_AHEAD)
+
+        @pl.when(h + AHEAD < HEADS)
+        def _():
+            send_cols(h + AHEAD)
+
+        @pl.when(h >= behind)
+        def _():
+            reduce_rows(h - behind)
+
+        @pl.when(h >= behind + 2)
+        def _():
+            relay_grad(h - behind - 2)
+
     def step(h):
+        @pl.when(h + AHEAD < HEADS)
+        def _():
+            pack_edges(h + AHEAD)
+
+        @pl.when(even)
+        def _():
+            columns(h, ROWS_BEHIND + 1)
+
         @pl.when(h + CORNERS_AHEAD < HEADS)
         def _():
             forward(h + CORNERS_AHEAD)
 
-        @pl.when(h + RELAY_AHEAD < HEADS)
-        def _():
-            relay_col(h + RELAY_AHEAD)
-
         @pl.when(h + AHEAD < HEADS)
         def _():
-            send_edges(h + AHEAD)
+            send_rows(h + AHEAD, (1, 2))
 
         for a in range(3):
             if a != 1:
@@ -383,23 +418,24 @@
             if a != 1:
                 send_grad_rows(h, a // 2)
 
-        @pl.when(h >= ROWS_BEHIND)
-        def _():
-            reduce_rows(h - ROWS_BEHIND)
-
-        @pl.when(h >= RELAY_BEHIND)
-        def _():
-            relay_grad(h - RELAY_BEHIND)
+        @pl.when(jnp.logical_not(even))
+        def _():
+            columns(h, ROWS_BEHIND)
 
         @pl.when(h >= BEHIND)
         def _():
             finish(h - BEHIND)
 
     loop(step)
+
+    @pl.when(even)
+    def _():
+        reduce_rows(HEADS - ROWS_BEHIND - 1)
+        relay_grad(HEADS - ROWS_BEHIND - 3)
+
     for h in range(HEADS - ROWS_BEHIND, HEADS):
         reduce_rows(h)
-
-    for h in range(HEADS - RELAY_BEHIND, HEADS):
+    for h in range(HEADS - ROWS_BEHIND - 2, HEADS):
         relay_grad(h)
     for h in range(HEADS - BEHIND, HEADS):
         finish(h)

time: 112 us -> 112 us (level)
  no operation moved by 1% of the time
where the time goes in v4:
time: 112 us
  Pallas kernels  111 us (99%)
    pallas_call x1, Pallas kernels, per_device(): pl.pallas_call(functools.partial(kernel, size_a, size_w), out_shape=[pltp...  109 us
    pallas_call x1, Pallas kernels, per_device(): pl.pallas_call(write_out, out_shape=[jax.ShapeDtypeStruct((4, 3, 32, HEAD...  2.31 us

profile of v4, /device:TPU:28, one launch (start us, length us, event | category | flops | bytes accessed | tf_op | source)
XLA Modules:
  0.0 112.0 jit_solution(6852212274401209855)
XLA Ops:
  0.6 109.0 %shard_map.84 = (bf16[4,3,32,1536]{3,2,1,0:T(8,128)(2,1)S(1)}, bf16[4,3,32,1536]{3,2,1,0:T(8,128)(2,1)S(1)}, bf16[4,3,32,1536]{3,2,1,0:T(8,128)(2,1)S(1)}, bf16[4,3,32,1536]{3,2,1,0:T(8,128)(2,1)S(1)}) custom-call(s32[3,2,4]{2,1,0:T(2,128)} %reach.1, bf16[4,3,32,1536]{3,2,1,0:T(8,128)(2,1)} %bitcast.8, bf16[4,3,32,1536]{3,2,1,0:T(8,128)(2,1)} %bitcast.9, ...), custom_call_target="tpu_custom_call" | custom-call | tf_op jit(solution)/shard_map/pallas_call | solution.py:489
  109.7 2.3 %shard_map.85 = (bf16[4,3,32,1536]{3,2,1,0:T(8,128)(2,1)}, bf16[4,3,32,1536]{3,2,1,0:T(8,128)(2,1)}, bf16[4,3,32,1536]{3,2,1,0:T(8,128)(2,1)}, bf16[4,3,32,1536]{3,2,1,0:T(8,128)(2,1)}) custom-call(bf16[4,3,32,1536]{3,2,1,0:T(8,128)(2,1)S(1)} %get-tuple-element.12.refs_0_, bf16[4,3,32,1536]{3,2,1,0:T(8,128)(2,1)S(1)} %get-tuple-element.13.refs_1_, ...), custom_call_target="tpu_custom_call" | custom-call | tf_op jit(solution)/shard_map/pallas_call | solution.py:522

commit v5 on v3

--- a/solution.py
+++ b/solution.py
@@ -108,6 +108,29 @@
         def _():
             ref = kall.at[h, :, 2 * j : 2 * j + 2, 4 * s]
             remote(ref, ref, ss2.at[h, s, j], rs2.at[h, s, j], ends[s][1]).wait_recv()
+
+    def alone(s, half):
+        return crossed[s] & jnp.logical_not(sides[half][0])
+
+    def part_of(ref, half):
+        return ref.at[:, 2 - 2 * half : 4 - 2 * half]
+
+    def lone_row_copy(h, s, half):
+        return remote(
+            part_of(g3s.at[h, s, half], half), part_of(g3r.at[h, 1 - s, half], half),
+            ss3.at[h, s, half], rs3.at[h, 1 - s, half], ends[s][1],
+        )
+
+    def for_grad_rows(s, lone, full):
+        for half in range(2):
+
+            @pl.when(ends[s][0] & alone(s, half))
+            def _():
+                lone(half)
+
+            @pl.when(ends[s][0] & jnp.logical_not(alone(s, half)))
+            def _():
+                full(half)
 
     def grad_row_copy(h, s, half):
         moved = crossed[s] & sides[half][0]
@@ -317,22 +340,29 @@
                     acc[h, kv, 6:8, row] += two[1][:, i]
 
     def send_grad_rows(h, s):
-        @pl.when(ends[s][0])
-        def _():
-            for half in range(2):
-                grad_row_copy(h, s, half).start()
+        for_grad_rows(s, lambda half: lone_row_copy(h, s, half).start(), lambda half: grad_row_copy(h, s, half).start())
 
     def reduce_rows(h):
         for s in range(2):
             row = 2 * s
 
+            def arrived(half, ref):
+                remote(ref, ref, ss3.at[h, s, half], rs3.at[h, s, half], ends[s][1]).wait_recv()
+
+            for_grad_rows(
+                s,
+                lambda half: arrived(half, part_of(g3r.at[h, s, half], half)),
+                lambda half: arrived(half, g3r.at[h, s, half]),
+            )
+            for half, (there, _) in enumerate(sides):
+
+                @pl.when(ends[s][0] & there)
+                def _():
+                    units = slice(6 * half, 6 * half + 2)
+                    acc[h, :, units, row] += g3r[h, s, half, :, 2 * half : 2 * half + 2].astype(F32)
+
             @pl.when(ends[s][0])
             def _():
-                for half in range(2):
-                    ref = g3r.at[h, s, half]
-                    remote(ref, ref, ss3.at[h, s, half], rs3.at[h, s, half], ends[s][1]).wait_recv()
-                acc[h, :, 0:2, row] += g3r[h, s, 0, :, 0:2].astype(F32)
-                acc[h, :, 6:8, row] += g3r[h, s, 1, :, 2:4].astype(F32)
                 x = [jnp.concatenate([g3r[h, s, 0, kv, 2:4], g3r[h, s, 1, kv, 0:2]]).reshape(128, D) for kv in range(2)]
                 for kv, y in enumerate(permute(perm, x[0], x[1])):
                     acc[h, kv, 2:6, row] += y.reshape(4, 32, D)
@@ -427,10 +457,9 @@
                 def _():
                     row_copy(h, s, j).wait_send()
 
-            @pl.when(ends[s][0])
-            def _():
-                for half in range(2):
-                    grad_row_copy(h, s, half).wait_send()
+            for_grad_rows(
+                s, lambda half: lone_row_copy(h, s, half).wait_send(), lambda half: grad_row_copy(h, s, half).wait_send()
+            )
 
     loop(drain)
 

time: 112 us -> 108 us (0.964); the launches traced: 112 us -> 106 us
  Pallas kernels: 111 us -> 105 us
    pallas_call x1, Pallas kernels: 109 us -> 103 us  [per_device(): pl.pallas_call(functools.partial(kernel, size_a, size_w), out_shape=[pltp...]
where the time goes in v5:
time: 108 us; the launch traced here: 106 us
  Pallas kernels  105 us (97%)
    pallas_call x1, Pallas kernels, per_device(): pl.pallas_call(functools.partial(kernel, size_a, size_w), out_shape=[pltp...  103 us
    pallas_call x1, Pallas kernels, per_device(): pl.pallas_call(write_out, out_shape=[jax.ShapeDtypeStruct((4, 3, 32, HEAD...  2.31 us

profile of v5, /device:TPU:28, one launch (start us, length us, event | category | flops | bytes accessed | tf_op | source)
XLA Modules:
  0.0 105.9 jit_solution(14903371488640041792)
XLA Ops:
  0.6 103.0 %shard_map.84 = (bf16[4,3,32,1536]{3,2,1,0:T(8,128)(2,1)S(1)}, bf16[4,3,32,1536]{3,2,1,0:T(8,128)(2,1)S(1)}, bf16[4,3,32,1536]{3,2,1,0:T(8,128)(2,1)S(1)}, bf16[4,3,32,1536]{3,2,1,0:T(8,128)(2,1)S(1)}) custom-call(s32[3,2,4]{2,1,0:T(2,128)} %reach.1, bf16[4,3,32,1536]{3,2,1,0:T(8,128)(2,1)} %bitcast.8, bf16[4,3,32,1536]{3,2,1,0:T(8,128)(2,1)} %bitcast.9, ...), custom_call_target="tpu_custom_call" | custom-call | tf_op jit(solution)/shard_map/pallas_call | solution.py:482
  103.6 2.3 %shard_map.85 = (bf16[4,3,32,1536]{3,2,1,0:T(8,128)(2,1)}, bf16[4,3,32,1536]{3,2,1,0:T(8,128)(2,1)}, bf16[4,3,32,1536]{3,2,1,0:T(8,128)(2,1)}, bf16[4,3,32,1536]{3,2,1,0:T(8,128)(2,1)}) custom-call(bf16[4,3,32,1536]{3,2,1,0:T(8,128)(2,1)S(1)} %get-tuple-element.12.refs_0_, bf16[4,3,32,1536]{3,2,1,0:T(8,128)(2,1)S(1)} %get-tuple-element.13.refs_1_, ...), custom_call_target="tpu_custom_call" | custom-call | tf_op jit(solution)/shard_map/pallas_call | solution.py:515

commit v6 on v5

--- a/solution.py
+++ b/solution.py
@@ -12,12 +12,12 @@
 TS = 4
 D = 128
 MESH = pl.DeviceIdType.MESH
-AHEAD = 7
-RELAY_AHEAD = 5
+AHEAD = 9
+RELAY_AHEAD = 6
 CORNERS_AHEAD = 3
-ROWS_BEHIND = 2
-RELAY_BEHIND = 4
-BEHIND = 6
+ROWS_BEHIND = 3
+RELAY_BEHIND = 6
+BEHIND = 9
 NEGATIVE = -1e30
 SCALE = 1.0 / math.sqrt(D)
 LOG2E = 1.4426950408889634

time: 108 us -> 106 us (0.981)
    pallas_call x1, Pallas kernels: 103 us -> 102 us  [per_device(): pl.pallas_call(functools.partial(kernel, size_a, size_w), out_shape=[pltp...]
where the time goes in v6:
time: 106 us; the launch traced here: 105 us
  Pallas kernels  104 us (98%)
    pallas_call x1, Pallas kernels, per_device(): pl.pallas_call(functools.partial(kernel, size_a, size_w), out_shape=[pltp...  102 us
    pallas_call x1, Pallas kernels, per_device(): pl.pallas_call(write_out, out_shape=[jax.ShapeDtypeStruct((4, 3, 32, HEAD...  2.31 us

profile of v6, /device:TPU:28, one launch (start us, length us, event | category | flops | bytes accessed | tf_op | source)
XLA Modules:
  0.0 104.6 jit_solution(16350301330455253626)
XLA Ops:
  0.6 101.7 %shard_map.84 = (bf16[4,3,32,1536]{3,2,1,0:T(8,128)(2,1)S(1)}, bf16[4,3,32,1536]{3,2,1,0:T(8,128)(2,1)S(1)}, bf16[4,3,32,1536]{3,2,1,0:T(8,128)(2,1)S(1)}, bf16[4,3,32,1536]{3,2,1,0:T(8,128)(2,1)S(1)}) custom-call(s32[3,2,4]{2,1,0:T(2,128)} %reach.1, bf16[4,3,32,1536]{3,2,1,0:T(8,128)(2,1)} %bitcast.8, bf16[4,3,32,1536]{3,2,1,0:T(8,128)(2,1)} %bitcast.9, ...), custom_call_target="tpu_custom_call" | custom-call | tf_op jit(solution)/shard_map/pallas_call | solution.py:482
  102.3 2.3 %shard_map.85 = (bf16[4,3,32,1536]{3,2,1,0:T(8,128)(2,1)}, bf16[4,3,32,1536]{3,2,1,0:T(8,128)(2,1)}, bf16[4,3,32,1536]{3,2,1,0:T(8,128)(2,1)}, bf16[4,3,32,1536]{3,2,1,0:T(8,128)(2,1)}) custom-call(bf16[4,3,32,1536]{3,2,1,0:T(8,128)(2,1)S(1)} %get-tuple-element.12.refs_0_, bf16[4,3,32,1536]{3,2,1,0:T(8,128)(2,1)S(1)} %get-tuple-element.13.refs_1_, ...), custom_call_target="tpu_custom_call" | custom-call | tf_op jit(solution)/shard_map/pallas_call | solution.py:515

commit v7 on v6

--- a/solution.py
+++ b/solution.py
@@ -12,12 +12,12 @@
 TS = 4
 D = 128
 MESH = pl.DeviceIdType.MESH
-AHEAD = 9
+AHEAD = 10
 RELAY_AHEAD = 6
 CORNERS_AHEAD = 3
 ROWS_BEHIND = 3
-RELAY_BEHIND = 6
-BEHIND = 9
+RELAY_BEHIND = 7
+BEHIND = 10
 NEGATIVE = -1e30
 SCALE = 1.0 / math.sqrt(D)
 LOG2E = 1.4426950408889634
@@ -52,15 +52,15 @@
     carried = jnp.where(parity == 1, ring, rings - 1 - ring)
     middle = (ia >= half_a - 2) & (ia < half_a + 2)
 
-    def chosen(k, part, fewer):
-        n = part * HEADS // rings - jnp.where(middle & (part > 0), fewer, 0)
+    def chosen(k, part, fewer, more):
+        n = part * HEADS // rings - jnp.where(middle & (part > 0), fewer, 0) + more
         return (k * n) % HEADS >= HEADS - n
 
     def relayed_col(h, part):
-        return chosen(h, part, jnp.where(part >= 2, 1, 0))
+        return chosen(h, part, jnp.where(part >= 2, 1, 0), jnp.where(part == 3, 1, 0))
 
     def relayed_grad(h, part):
-        return chosen(HEADS - 1 - h, part, jnp.where(part >= 3, 2, 1))
+        return chosen(HEADS - 1 - h, part, jnp.where(part >= 3, 2, 1), 0)
 
     def lanes(h):
         return pl.ds(pl.multiple_of(h * D, D), D)
@@ -252,7 +252,7 @@
         send_rows(h, (1, 2))
         send(col_copy, col_relay_in, relayed_col, h)
 
-    for h in range(3):
+    for h in range(4):
         send_edges(h)
 
     shape = (6, 3, 32, 128)
@@ -386,8 +386,8 @@
         relay_col(h)
         if h < CORNERS_AHEAD:
             forward(h)
-        if h + 3 < AHEAD:
-            send_edges(h + 3)
+        if h + 4 < AHEAD:
+            send_edges(h + 4)
 
     loads[2].wait()
     loads[3].wait()

time: 106 us -> 108 us (1.019); the launches traced: 105 us -> 108 us
  Pallas kernels: 104 us -> 108 us
    pallas_call x1, Pallas kernels: 102 us -> 105 us  [per_device(): pl.pallas_call(functools.partial(kernel, size_a, size_w), out_shape=[pltp...]
where the time goes in v7:
time: 108 us
  Pallas kernels  108 us (100%)
    pallas_call x1, Pallas kernels, per_device(): pl.pallas_call(functools.partial(kernel, size_a, size_w), out_shape=[pltp...  105 us
    pallas_call x1, Pallas kernels, per_device(): pl.pallas_call(write_out, out_shape=[jax.ShapeDtypeStruct((4, 3, 32, HEAD...  2.31 us

profile of v7, /device:TPU:28, one launch (start us, length us, event | category | flops | bytes accessed | tf_op | source)
XLA Modules:
  0.0 108.2 jit_solution(10425179420092513190)
XLA Ops:
  0.6 105.2 %shard_map.84 = (bf16[4,3,32,1536]{3,2,1,0:T(8,128)(2,1)S(1)}, bf16[4,3,32,1536]{3,2,1,0:T(8,128)(2,1)S(1)}, bf16[4,3,32,1536]{3,2,1,0:T(8,128)(2,1)S(1)}, bf16[4,3,32,1536]{3,2,1,0:T(8,128)(2,1)S(1)}) custom-call(s32[3,2,4]{2,1,0:T(2,128)} %reach.1, bf16[4,3,32,1536]{3,2,1,0:T(8,128)(2,1)} %bitcast.8, bf16[4,3,32,1536]{3,2,1,0:T(8,128)(2,1)} %bitcast.9, ...), custom_call_target="tpu_custom_call" | custom-call | tf_op jit(solution)/shard_map/pallas_call | solution.py:482
  105.9 2.3 %shard_map.85 = (bf16[4,3,32,1536]{3,2,1,0:T(8,128)(2,1)}, bf16[4,3,32,1536]{3,2,1,0:T(8,128)(2,1)}, bf16[4,3,32,1536]{3,2,1,0:T(8,128)(2,1)}, bf16[4,3,32,1536]{3,2,1,0:T(8,128)(2,1)}) custom-call(bf16[4,3,32,1536]{3,2,1,0:T(8,128)(2,1)S(1)} %get-tuple-element.12.refs_0_, bf16[4,3,32,1536]{3,2,1,0:T(8,128)(2,1)S(1)} %get-tuple-element.13.refs_1_, ...), custom_call_target="tpu_custom_call" | custom-call | tf_op jit(solution)/shard_map/pallas_call | solution.py:515

commit v8 on v6

--- a/solution.py
+++ b/solution.py
@@ -15,9 +15,9 @@
 AHEAD = 9
 RELAY_AHEAD = 6
 CORNERS_AHEAD = 3
-ROWS_BEHIND = 3
-RELAY_BEHIND = 6
-BEHIND = 9
+ROWS_BEHIND = 4
+RELAY_BEHIND = 7
+BEHIND = 10
 NEGATIVE = -1e30
 SCALE = 1.0 / math.sqrt(D)
 LOG2E = 1.4426950408889634

time: 106 us -> 106 us (level)
  the two profiles are of different devices: /device:TPU:28 before, /device:TPU:20 now
where the time goes in v8:
time: 106 us
  Pallas kernels  106 us (100%)
    pallas_call x1, Pallas kernels, per_device(): pl.pallas_call(functools.partial(kernel, size_a, size_w), out_shape=[pltp...  103 us
    pallas_call x1, Pallas kernels, per_device(): pl.pallas_call(write_out, out_shape=[jax.ShapeDtypeStruct((4, 3, 32, HEAD...  2.31 us

profile of v8, /device:TPU:20, one launch (start us, length us, event | category | flops | bytes accessed | tf_op | source)
XLA Modules:
  0.0 106.3 jit_solution(4125135122858684888)
XLA Ops:
  0.6 103.3 %shard_map.84 = (bf16[4,3,32,1536]{3,2,1,0:T(8,128)(2,1)S(1)}, bf16[4,3,32,1536]{3,2,1,0:T(8,128)(2,1)S(1)}, bf16[4,3,32,1536]{3,2,1,0:T(8,128)(2,1)S(1)}, bf16[4,3,32,1536]{3,2,1,0:T(8,128)(2,1)S(1)}) custom-call(s32[3,2,4]{2,1,0:T(2,128)} %reach.1, bf16[4,3,32,1536]{3,2,1,0:T(8,128)(2,1)} %bitcast.8, bf16[4,3,32,1536]{3,2,1,0:T(8,128)(2,1)} %bitcast.9, ...), custom_call_target="tpu_custom_call" | custom-call | tf_op jit(solution)/shard_map/pallas_call | solution.py:482
  104.0 2.3 %shard_map.85 = (bf16[4,3,32,1536]{3,2,1,0:T(8,128)(2,1)}, bf16[4,3,32,1536]{3,2,1,0:T(8,128)(2,1)}, bf16[4,3,32,1536]{3,2,1,0:T(8,128)(2,1)}, bf16[4,3,32,1536]{3,2,1,0:T(8,128)(2,1)}) custom-call(bf16[4,3,32,1536]{3,2,1,0:T(8,128)(2,1)S(1)} %get-tuple-element.12.refs_0_, bf16[4,3,32,1536]{3,2,1,0:T(8,128)(2,1)S(1)} %get-tuple-element.13.refs_1_, ...), custom_call_target="tpu_custom_call" | custom-call | tf_op jit(solution)/shard_map/pallas_call | solution.py:515

commit v9 on v6

--- a/solution.py
+++ b/solution.py
@@ -466,7 +466,7 @@
 
 def write_out(*refs):
     sources, outs, sem = refs[:4], refs[4:8], refs[8]
-    copies = [pltpu.make_async_copy(x.at[f], y.at[f], sem.at[n, f]) for n, (x, y) in enumerate(zip(sources, outs)) for f in range(4)]
+    copies = [pltpu.make_async_copy(x, y, sem.at[n]) for n, (x, y) in enumerate(zip(sources, outs))]
     for copy in copies:
         copy.start()
     for copy in copies:
@@ -517,7 +517,7 @@
         out_shape=[jax.ShapeDtypeStruct((4, 3, 32, HEADS * D), BF16)] * 4,
         in_specs=[pl.BlockSpec(memory_space=pltpu.VMEM)] * 4,
         out_specs=[any_spec] * 4,
-        scratch_shapes=[pltpu.SemaphoreType.DMA((4, 4))],
+        scratch_shapes=[pltpu.SemaphoreType.DMA((4,))],
         compiler_params=pltpu.CompilerParams(vmem_limit_bytes=8 * 1024 * 1024),
     )(*(pltpu.with_memory_space_constraint(x, pltpu.VMEM) for x in results))
     return tuple(x.reshape(shape) for x in outs)

time: 106 us -> 106 us (level)
  no operation moved by 1% of the time
where the time goes in v9:
time: 106 us; the launch traced here: 105 us
  Pallas kernels  104 us (98%)
    pallas_call x1, Pallas kernels, per_device(): pl.pallas_call(functools.partial(kernel, size_a, size_w), out_shape=[pltp...  102 us
    pallas_call x1, Pallas kernels, per_device(): pl.pallas_call(write_out, out_shape=[jax.ShapeDtypeStruct((4, 3, 32, HEAD...  2.22 us

profile of v9, /device:TPU:28, one launch (start us, length us, event | category | flops | bytes accessed | tf_op | source)
XLA Modules:
  0.0 104.5 jit_solution(6915180229538894848)
XLA Ops:
  0.6 101.7 %shard_map.84 = (bf16[4,3,32,1536]{3,2,1,0:T(8,128)(2,1)S(1)}, bf16[4,3,32,1536]{3,2,1,0:T(8,128)(2,1)S(1)}, bf16[4,3,32,1536]{3,2,1,0:T(8,128)(2,1)S(1)}, bf16[4,3,32,1536]{3,2,1,0:T(8,128)(2,1)S(1)}) custom-call(s32[3,2,4]{2,1,0:T(2,128)} %reach.1, bf16[4,3,32,1536]{3,2,1,0:T(8,128)(2,1)} %bitcast.8, bf16[4,3,32,1536]{3,2,1,0:T(8,128)(2,1)} %bitcast.9, ...), custom_call_target="tpu_custom_call" | custom-call | tf_op jit(solution)/shard_map/pallas_call | solution.py:482
  102.3 2.2 %shard_map.85 = (bf16[4,3,32,1536]{3,2,1,0:T(8,128)(2,1)}, bf16[4,3,32,1536]{3,2,1,0:T(8,128)(2,1)}, bf16[4,3,32,1536]{3,2,1,0:T(8,128)(2,1)}, bf16[4,3,32,1536]{3,2,1,0:T(8,128)(2,1)}) custom-call(bf16[4,3,32,1536]{3,2,1,0:T(8,128)(2,1)S(1)} %get-tuple-element.12.refs_0_, bf16[4,3,32,1536]{3,2,1,0:T(8,128)(2,1)S(1)} %get-tuple-element.13.refs_1_, ...), custom_call_target="tpu_custom_call" | custom-call | tf_op jit(solution)/shard_map/pallas_call | solution.py:515
